TPU v7x, 32 devices: a whole 2x2x4 slice. The times are simulated.
32 devices in a mesh: row: 8 (over z, x), reach: 4 (over y, core).
Axes of the slice: x: 2, y: 2, z: 4, core: 2. Of those that a mesh axis runs over, the one named last changes fastest.
Arguments:
- basis: bfloat16 [65536, 128], P(('row', 'reach')), may hold values from -6 to 6
- near_cols: int32 [1024, 7], P(('row', 'reach')), may hold values from 0 to 127, as said below
- near_count: int32 [1024], P(('row', 'reach')), may hold values from 1 to 7
- near_blocks: bfloat16 [1024, 7, 4096], P(('row', 'reach')), may hold values from -0.25 to 0.25
- marker_rows: int32 [512], P(('row', 'reach')), may hold values from 0 to 31
- marker_groups: int32 [512], P(('row', 'reach')), may hold values from 0 to 63, as said below
- marker_count: int32 [32], P(('row', 'reach')), may hold values from 2 to 16
- marker_weights: bfloat16 [512, 4096], P(('row', 'reach')), may hold values from -0.75 to 0.75
- stiffness: float32 [4096], replicated, may hold values from 0.5 to 4
Outputs:
- qfactor: float32 [65536, 128], P(('row', 'reach'))
- rfactor: float32 [128, 128], replicated
Inputs may be any that keep to these rules, and one draw needn't show every extreme that they name: `near_cols`: the first stored block of each block row is the block row itself. `marker_groups`: slot 0 of slab s names group ((64 * s) // 32 + 64 // 2) % 64; slot 1 names (64 * s) // 32; every other slot names that group or the one after it, never beyond 64 - 1.
All inputs are finite; a program needn't handle non-finite values.
Results may differ from a plain program's by a relative error of at most 0.0025.
Values may be sent and summed in bfloat16 or wider, within the bound.
A program may use at most 64 MiB of HBM per device.

v0:
```python
import jax
import jax.numpy as jnp
from jax import lax
from jax.sharding import PartitionSpec as P

BS = 64
NG = 64


def force_of(sums, stiffness):
    scale = lax.rsqrt(1.0 + jnp.mean(sums * sums, axis=1, keepdims=True))
    return (stiffness[:, None] * sums * scale).astype(jnp.bfloat16)


def local(
    basis,
    near_cols,
    near_count,
    near_blocks,
    marker_rows,
    marker_groups,
    marker_count,
    marker_weights,
    stiffness,
):
    slab, stored = near_cols.shape
    width = basis.shape[1]
    side = BS
    slots = marker_rows.shape[0]
    groups = NG
    markers = groups * side
    hp = lax.Precision.HIGHEST
    own = basis.reshape(slab, side, width)
    weights = marker_weights.reshape(slots, side, side)
    mlive = jnp.arange(slots, dtype=jnp.int32) < marker_count[0]
    picked = own[marker_rows]
    partial_value = jnp.einsum("mcj,mcd->mjd", weights, picked, preferred_element_type=jnp.float32)
    partial_flat = partial_value.reshape(slots, side * width)
    onehot = (marker_groups[None, :] == jnp.arange(groups, dtype=jnp.int32)[:, None]) & mlive[
        None, :
    ]
    local_sums = jnp.dot(onehot.astype(jnp.float32), partial_flat, precision=hp).reshape(
        markers, width
    )
    totals = lax.psum(local_sums, ("row", "reach"))
    force = force_of(totals, stiffness)
    force_rows = jnp.dot(
        onehot.T.astype(jnp.bfloat16),
        force.reshape(groups, side * width),
        preferred_element_type=jnp.float32,
    )
    group_basis = lax.all_gather(basis, "reach", axis=0, tiled=True).reshape(-1, side, width)
    live = jnp.arange(stored, dtype=jnp.int32)[None, :] < near_count[:, None]
    fetched = jnp.where(live[:, :, None, None], group_basis[near_cols], jnp.zeros((), jnp.bfloat16))
    blocks = near_blocks.reshape(slab, stored, side, side)
    near = jnp.einsum("bkrc,bkcd->brd", blocks, fetched, preferred_element_type=jnp.float32)
    force_rows = force_rows.astype(jnp.bfloat16).reshape(slots, side, width)
    contrib = jnp.einsum("mcj,mjd->mcd", weights, force_rows, preferred_element_type=jnp.float32)
    rowhot = (
        (marker_rows[None, :] == jnp.arange(slab, dtype=jnp.int32)[:, None]) & mlive[None, :]
    ).astype(jnp.float32)
    spread = jnp.dot(rowhot, contrib.reshape(slots, side * width), precision=hp).reshape(
        slab, side, width
    )
    image = (near + spread).reshape(slab * side, width)
    gram = lax.psum(jnp.dot(image.T, image, precision=hp), ("row", "reach"))
    lower = jnp.linalg.cholesky(gram)
    solved = jax.scipy.linalg.solve_triangular(lower, image.T, lower=True)
    total_rows = slab * side * lax.axis_size(("row", "reach"))
    root = jnp.sqrt(jnp.float32(total_rows))
    return (solved.T * root, lower.T / root)


def solution(mesh):
    return jax.shard_map(
        local,
        mesh=mesh,
        in_specs=(
            P(("row", "reach"), None),
            P(("row", "reach"), None),
            P(("row", "reach")),
            P(("row", "reach"), None, None),
            P(("row", "reach")),
            P(("row", "reach")),
            P(("row", "reach")),
            P(("row", "reach"), None),
            P(),
        ),
        out_specs=(P(("row", "reach"), None), P()),
        check_vma=False,
    )
```

profile of v0, /device:TPU:0, one launch (start us, length us, event | category | flops | bytes accessed | tf_op | source)
XLA Modules:
  0.0 330.2 jit_solution(2423852829834290028)
XLA Ops:
  8.7 0.7 compare_select_fusion.1
  9.4 1.2 reshape.85
  10.5 1.6 gather_fusion.1
  12.5 1.8 fusion.16
  14.3 1.6 reshape.87
  16.7 0.6 copy-done.1
  17.4 4.9 %reshape.83 = bf16[32,7,64,64]{3,2,0,1:T(8,128)(2,1)} reshape(bf16[32,7,4096]{2,0,1:T(8,128)(2,1)S(1)} %copy-done.1) | data formatting | bytes 3670016 | tf_op jit(solution)/shard_map/reshape | solution.py:55
  22.4 137.9 %all-reduce.3.cloned.1.call-done = f32[4096,128]{1,0:T(8,128)} async-done(((f32[4096,128]{1,0:T(8,128)}), f32[4096,128]{1,0:T(8,128)}) %all-reduce.3.cloned.1.call-update) | async-done | bytes 2097168 | tf_op jit(solution)/shard_map/psum | solution.py:45
  160.3 2.4 multiply_reduce_fusion
  162.7 2.3 multiply_convert_fusion
  165.0 0.7 reshape.88
  166.3 0.9 fusion.19
  167.2 4.5 %gather_fusion = bf16[224,64,128]{2,1,0:T(8,128)(2,1)} fusion(bf16[128,64,128]{2,1,0:T(8,128)(2,1)} %bitcast.62, s32[1024]{0:T(1024)S(1)} %pad_clamp_fusion.1), kind=kCustom, calls=%fused_computation | custom fusion | bytes 7340928 | tf_op jit(solution)/shard_map/gather | solution.py:54
  171.8 4.6 %fusion.10 = f32[32,64,128]{2,1,0:T(8,128)S(1)} fusion(bf16[32,7,64,128]{3,2,1,0:T(8,128)(2,1)} %bitcast.63, pred[32,7]{1,0:T(8,128)(4,1)S(1)} %iota_compare_fusion.3, bf16[32,7,64,64]{3,2,0,1:T(8,128)(2,1)} %reshape.83, f32[32,64,128]{2,0,1:T(8,128)S(1)} %fusion.19), kind=kOutput, calls=%fused_computation.12 | convolution fusion | flops 236978176 | bytes 7602400 | tf_op jit(solution)/shard_map/bkrc,bkcd->brd/dot_general | solution.py:56
  176.4 2.4 convolution_bitcast_fusion
  178.9 116.6 %all-reduce.5.cloned.1.call-done = f32[128,128]{0,1:T(8,128)} async-done(((f32[128,128]{0,1:T(8,128)}), f32[128,128]{0,1:T(8,128)}) %all-reduce.5.cloned.1.call-update) | async-done | bytes 65552 | tf_op jit(solution)/shard_map/psum | solution.py:66
  295.4 0.9 copy.23
  296.4 0.9 fusion.23
  297.2 11.7 %cholesky.16 = f32[128,128]{1,0:T(8,128)S(1)} custom-call(f32[128,128]{1,0:T(8,128)S(1)} %fusion.23), custom_call_target="Cholesky" | custom-call | tf_op jit(solution)/shard_map/jit(cholesky)/cholesky | solution.py:67
  309.0 0.6 compare_reduce_fusion
  309.6 0.7 multiply_bitcast_fusion
  310.3 0.7 copy.24
  311.0 9.8 %custom-call.7 = f32[1,128,128]{1,2,0:T(8,128)S(1)} custom-call(f32[1,128,128]{2,1,0:T(8,128)S(1)} %get-tuple-element.7), custom_call_target="InvertDiagBlocksLowerTriangular" | custom-call | tf_op jit(solution)/shard_map/jit(_solve_triangular)/triangular_solve | solution.py:68
  320.8 1.9 convolution_multiply_fusion
  (33 shorter events, 1.9 us)
Async XLA Ops:
  8.0 152.3 %all-reduce.3.cloned.1.call-start = ((), (), s32[]{:S(2)}) async-start(), calls=%async_computation.1 | async-start | bytes 4194304 | tf_op jit(solution)/shard_map/psum | solution.py:45
  15.9 0.7 copy-start.3
  15.9 1.5 copy-start.1
  15.9 151.3 %all-gather.2.cloned.1.call-start = ((), (), s32[]{:S(2)}) async-start(), calls=%async_computation | async-start | bytes 2621440 | tf_op jit(solution)/shard_map/all_gather | solution.py:52
  16.5 279.0 %all-reduce.5.cloned.1.call-start = ((), (), s32[]{:S(2)}) async-start(), calls=%async_computation.2 | async-start | bytes 131072 | tf_op jit(solution)/shard_map/psum | solution.py:66
  17.4 5.0 %copy-start.6 = (s32[32]{0:T(128)S(1)}, s32[32]{0:T(128)}, u32[]{:S(2)}) copy-start(s32[32]{0:T(128)} %param.11) | copy-start | bytes 388
  22.3 140.4 %copy-start.2 = (f32[4096]{0:T(1024)S(1)}, f32[4096]{0:T(1024)}, u32[]{:S(2)}) copy-start(f32[4096]{0:T(1024)} %param.17) | copy-start | bytes 49156
  160.3 2.4 copy-start
  162.7 3.0 copy-start.4
  165.0 1.3 copy-start.5
Sparse Core Ops, SparseCore 0:
  16.0 144.2 all-reduce.2
  179.0 116.4 all-reduce.4
Sparse Core Ops, SparseCore 1:
  17.9 25.8 all-gather.1
where the time goes:
time: 332 us; the launch traced here: 330 us
  waiting for transfers between devices  255 us (77%)
  other arithmetic  29.1 us (9%)
  local copies, waits for them, and re-layouts  17.1 us (5%)
  between operations  16.3 us (5%)
  matrix products  12.5 us (4%)
    psum x1, waiting for transfers between devices, local(): totals = lax.psum(local_sums, ('row', 'reach'))  138 us
    psum x1, waiting for transfers between devices, local(): gram = lax.psum(jnp.dot(image.T, image, precision=hp), ('row', 'reach'))  117 us
    another operation x3, other arithmetic, local(): lower = jnp.linalg.cholesky(gram)  12.4 us
    another operation x1, other arithmetic, local(): solved = jax.scipy.linalg.solve_triangular(lower, image.T, lower=True)  9.81 us
  transfers between devices with their start and end apart: 3, of which 2 were waited for; matrix products, arithmetic and copies ran while one was open for 4% of the time, Pallas kernels for 0%

commit v1 on v0

v1 whole, which is shorter than its diff:
```python
import functools

import jax
import jax.numpy as jnp
from jax import lax
from jax.experimental import pallas as pl
from jax.experimental.pallas import tpu as pltpu
from jax.sharding import PartitionSpec as P

BS = 64
NG = 64
CHUNKS = 4
HP = lax.Precision.HIGHEST
MESH = pl.DeviceIdType.MESH
VM = pl.BlockSpec(memory_space=pltpu.VMEM)
SM = pl.BlockSpec(memory_space=pltpu.SMEM)


def dot(a, b, da, db, precision=None):
    return lax.dot_general(
        a, b, (((da,), (db,)), ((), ())), precision=precision, preferred_element_type=jnp.float32
    )


def image_kernel(
    rows,
    reach,
    cols,
    mrow,
    code,
    basis,
    blocks,
    weights,
    stiff,
    image,
    gram,
    grp,
    sums,
    other,
    force,
    contrib,
    part,
    buf1,
    quarter,
    buf2,
    local_sem,
    sib_send,
    sib_recv,
    y_send,
    y_recv,
    f_send,
    f_recv,
    m_send,
    m_recv,
    s1,
    r1,
    s2,
    r2,
    s3,
    r3,
):
    z = lax.axis_index("row")
    r = lax.axis_index("reach")
    slab, side, width = basis.shape
    stored = blocks.shape[2] // side
    slots = weights.shape[0]
    core = lax.rem(r, 2)
    sib = r + 1 - 2 * core
    far = lax.rem(r + 2, reach)

    barrier = pltpu.get_barrier_semaphore()
    for d in range(1, reach):
        pl.semaphore_signal(
            barrier, inc=1, device_id=(z, lax.rem(r + d, reach)), device_id_type=MESH
        )
    for d in range(1, rows):
        pl.semaphore_signal(
            barrier, inc=1, device_id=(lax.rem(z + d, rows), r), device_id_type=MESH
        )
    pl.semaphore_wait(barrier, reach + rows - 2)

    def remote(src, dst, ss, rs, dev):
        return pltpu.make_async_remote_copy(
            src_ref=src, dst_ref=dst, send_sem=ss, recv_sem=rs, device_id=dev, device_id_type=MESH
        )

    step = slab // CHUNKS
    to_far = []
    for c in range(CHUNKS):
        cp = remote(
            basis.at[pl.ds(c * step, step)],
            grp.at[pl.ds(r * slab + c * step, step)],
            y_send.at[c],
            y_recv.at[c],
            (z, far),
        )
        cp.start()
        to_far.append(cp)
    to_sib = remote(basis, grp.at[pl.ds(r * slab, slab)], sib_send, sib_recv, (z, sib))
    to_sib.start()
    own = pltpu.make_async_copy(basis, grp.at[pl.ds(r * slab, slab)], local_sem)
    own.start()
    grp[reach * slab] = jnp.zeros((side, width), grp.dtype)

    sums[...] = jnp.zeros_like(sums)

    def gather_step(m, carry):
        value = dot(weights[m], basis[mrow[m]], 0, 0)
        for g in range(3):
            sums[g] = sums[g] + jnp.where(code[m] == g, 1.0, 0.0) * value
        return carry

    lax.fori_loop(0, slots, gather_step, 0)
    swap = remote(
        sums.at[pl.ds(0, 2)], other, m_send, m_recv, (lax.rem(z + rows // 2, rows), r)
    )
    swap.start()

    def force_of(total, g):
        scale = lax.rsqrt(1.0 + jnp.mean(total * total, axis=1, keepdims=True))
        return (stiff[g] * total * scale).astype(jnp.bfloat16)

    force[2] = force_of(sums[2], 2)
    fwd = []
    for c in range(CHUNKS):
        to_far[c].wait_recv()
        place = pl.ds(far * slab + c * step, step)
        cp = remote(grp.at[place], grp.at[place], f_send.at[c], f_recv.at[c], (z, sib))
        cp.start()
        fwd.append(cp)
    swap.wait()
    force[0] = force_of(sums[0] + other[1], 0)
    force[1] = force_of(sums[1] + other[0], 1)

    def spread_step(m, carry):
        contrib[m] = dot(weights[m], force[jnp.minimum(code[m], 2)], 1, 0)
        return carry

    lax.fori_loop(0, slots, spread_step, 0)

    own.wait()
    to_sib.wait()
    for c in range(CHUNKS):
        to_far[c].wait_send()
        fwd[c].wait()

    def near_step(i, carry):
        fetched = jnp.concatenate([grp[cols[i * stored + k]] for k in range(stored)], axis=0)
        acc = dot(blocks[i], fetched, 1, 0)
        for m in range(slots):
            hit = jnp.where((mrow[m] == i) & (code[m] < 3), 1.0, 0.0)
            acc = acc + hit * contrib[m]
        image[pl.ds(pl.multiple_of(i * side, side), side)] = acc
        return carry

    lax.fori_loop(0, slab, near_step, 0)

    part[...] = jnp.zeros_like(part)

    def gram_step(i, carry):
        x = image[pl.ds(pl.multiple_of(i * 256, 256), 256)]
        part[...] += dot(x, x, 0, 0, HP).reshape(part.shape)
        return carry

    lax.fori_loop(0, slab * side // 256, gram_step, 0)

    first = []
    for d in range(1, reach):
        peer = lax.rem(r + d, reach)
        cp = remote(part.at[peer], buf1.at[d - 1], s1.at[d - 1], r1.at[d - 1], (z, peer))
        cp.start()
        first.append(cp)
    for cp in first:
        cp.wait()
    total = part[r]
    for d in range(reach - 1):
        total = total + buf1[d]
    quarter[...] = total
    second = []
    for d in range(1, rows):
        peer = lax.rem(z + d, rows)
        cp = remote(quarter, buf2.at[z], s2.at[d - 1], r2.at[d - 1], (peer, r))
        cp.start()
        second.append(cp)
    buf2[z] = total
    for cp in second:
        cp.wait()
    total = buf2[0]
    for d in range(1, rows):
        total = total + buf2[d]
    gram[r] = total
    third = []
    for d in range(1, reach):
        peer = lax.rem(r + d, reach)
        cp = remote(gram.at[r], gram.at[r], s3.at[d - 1], r3.at[d - 1], (z, peer))
        cp.start()
        third.append(cp)
    for cp in third:
        cp.wait()


def image_and_gram(
    rows,
    reach,
    basis,
    near_cols,
    near_count,
    near_blocks,
    marker_rows,
    marker_groups,
    marker_count,
    marker_weights,
    stiffness,
):
    slab, stored = near_cols.shape
    width = basis.shape[1]
    side = BS
    slots = marker_rows.shape[0]
    per = NG // (rows * reach)
    s = lax.axis_index(("row", "reach")).astype(jnp.int32)
    base = s * per
    away = lax.rem(base + NG // 2, NG)
    live = jnp.arange(stored, dtype=jnp.int32)[None, :] < near_count[:, None]
    cols = jnp.where(live, near_cols, reach * slab).reshape(-1)
    mlive = jnp.arange(slots, dtype=jnp.int32) < marker_count[0]
    code = jnp.where(
        marker_groups == base, 0, jnp.where(marker_groups == away, 1, 2)
    ).astype(jnp.int32)
    code = jnp.where(mlive, code, 3)
    blocks = (
        near_blocks.reshape(slab, stored, side, side)
        .transpose(0, 2, 1, 3)
        .reshape(slab, side, stored * side)
    )
    weights = marker_weights.reshape(slots, side, side)
    st = stiffness.reshape(NG, side)
    stiff = jnp.stack(
        [lax.dynamic_index_in_dim(st, g, 0, keepdims=False) for g in (base, away, base + 1)]
    )[:, :, None]
    q = width // reach
    f32, bf16 = jnp.float32, jnp.bfloat16
    dma = pltpu.SemaphoreType.DMA
    image, gram = pl.pallas_call(
        functools.partial(image_kernel, rows, reach),
        out_shape=(
            jax.ShapeDtypeStruct((slab * side, width), f32),
            jax.ShapeDtypeStruct((reach, q, width), f32),
        ),
        in_specs=[SM, SM, SM, VM, VM, VM, VM],
        out_specs=(VM, VM),
        scratch_shapes=[
            pltpu.VMEM((reach * slab + 1, side, width), bf16),
            pltpu.VMEM((3, side, width), f32),
            pltpu.VMEM((2, side, width), f32),
            pltpu.VMEM((3, side, width), bf16),
            pltpu.VMEM((slots, side, width), f32),
            pltpu.VMEM((reach, q, width), f32),
            pltpu.VMEM((reach - 1, q, width), f32),
            pltpu.VMEM((q, width), f32),
            pltpu.VMEM((rows, q, width), f32),
            dma,
            dma,
            dma,
            dma((CHUNKS,)),
            dma((CHUNKS,)),
            dma((CHUNKS,)),
            dma((CHUNKS,)),
            dma,
            dma,
            dma((reach - 1,)),
            dma((reach - 1,)),
            dma((rows - 1,)),
            dma((rows - 1,)),
            dma((reach - 1,)),
            dma((reach - 1,)),
        ],
        compiler_params=pltpu.CompilerParams(
            collective_id=0, has_side_effects=True, vmem_limit_bytes=40 * 1024 * 1024
        ),
    )(
        cols,
        marker_rows,
        code,
        basis.reshape(slab, side, width),
        blocks,
        weights,
        stiff,
    )
    return image, gram.reshape(width, width)


def factor_kernel(root, image, gram, qf, rf, work, full):
    n = gram.shape[0]
    row = lax.broadcasted_iota(jnp.int32, (n, n), 0)
    col = lax.broadcasted_iota(jnp.int32, (n, n), 1)
    work[:, :n] = gram[...]
    work[:, n:] = jnp.where(row == col, 1.0, 0.0)
    sub = lax.broadcasted_iota(jnp.int32, (8, n), 0)
    for p in range(0, n, 8):
        left = work[p : p + 8, :n]
        right = work[p : p + 8, n:]
        cs = [jnp.broadcast_to(left[:, p + j : p + j + 1], (8, n)) for j in range(8)]
        scale = jnp.zeros((8, n), jnp.float32)
        for j in range(8):
            piv = cs[j][j : j + 1, :]
            rs = lax.rsqrt(piv)
            rs = rs * (1.5 - 0.5 * piv * rs * rs)
            scale = jnp.where(sub == j, rs, scale)
            if j == 7:
                break
            mult = jnp.where(sub > j, cs[j] * (rs * rs), 0.0)
            for i in range(j + 1, 8):
                cs[i] = cs[i] - mult * cs[i][j : j + 1, :]
            left = left - mult * left[j : j + 1, :]
            right = right - mult * right[j : j + 1, :]
        left = left * scale
        right = right * scale
        full[p : p + 8, :n] = left
        full[p : p + 8, n:] = right
        if p + 8 < n:
            both = jnp.concatenate([left, right], axis=1)
            change = dot(left, both, 0, 0, HP)
            work[p + 8 :, :] = work[p + 8 :, :] - change[p + 8 :, :]
    rf[...] = jnp.where(col >= row, full[:, :n], 0.0) * (1.0 / root)
    inverse = full[:, n:] * root

    def step(i, carry):
        at = pl.ds(pl.multiple_of(i * 256, 256), 256)
        qf[at] = dot(image[at], inverse, 1, 1, HP)
        return carry

    lax.fori_loop(0, image.shape[0] // 256, step, 0)


def factor(image, gram, total_rows):
    n = gram.shape[0]
    f32 = jnp.float32
    return pl.pallas_call(
        functools.partial(factor_kernel, float(total_rows) ** 0.5),
        out_shape=(
            jax.ShapeDtypeStruct(image.shape, f32),
            jax.ShapeDtypeStruct((n, n), f32),
        ),
        in_specs=[VM, VM],
        out_specs=(VM, VM),
        scratch_shapes=[pltpu.VMEM((n, 2 * n), f32), pltpu.VMEM((n, 2 * n), f32)],
        compiler_params=pltpu.CompilerParams(vmem_limit_bytes=40 * 1024 * 1024),
    )(image, gram)


def pick(index, table):
    count = table.shape[0]
    hot = index[:, None] == jnp.arange(count, dtype=jnp.int32)[None, :]
    taken = jnp.dot(hot.astype(table.dtype), table.reshape(count, -1))
    return taken.reshape((index.shape[0],) + table.shape[1:])


def plain_image_and_gram(
    basis,
    near_cols,
    near_count,
    near_blocks,
    marker_rows,
    marker_groups,
    marker_count,
    marker_weights,
    stiffness,
):
    slab, stored = near_cols.shape
    width = basis.shape[1]
    side = BS
    slots = marker_rows.shape[0]
    groups = NG
    own = basis.reshape(slab, side, width)
    weights = marker_weights.reshape(slots, side, side)
    mlive = jnp.arange(slots, dtype=jnp.int32) < marker_count[0]
    picked = pick(marker_rows, own)
    partial_value = jnp.einsum("mcj,mcd->mjd", weights, picked, preferred_element_type=jnp.float32)
    onehot = (marker_groups[None, :] == jnp.arange(groups, dtype=jnp.int32)[:, None]) & mlive[
        None, :
    ]
    sums = jnp.dot(
        onehot.astype(jnp.float32), partial_value.reshape(slots, side * width), precision=HP
    ).reshape(groups * side, width)
    sums = lax.psum(sums, ("row", "reach"))
    scale = lax.rsqrt(1.0 + jnp.mean(sums * sums, axis=1, keepdims=True))
    force = (stiffness[:, None] * sums * scale).astype(jnp.bfloat16)
    force_rows = jnp.dot(
        onehot.T.astype(jnp.bfloat16),
        force.reshape(groups, side * width),
        preferred_element_type=jnp.float32,
    )
    group_basis = lax.all_gather(basis, "reach", axis=0, tiled=True).reshape(-1, side, width)
    live = jnp.arange(stored, dtype=jnp.int32)[None, :] < near_count[:, None]
    fetched = pick(jnp.where(live, near_cols, -1).reshape(-1), group_basis)
    fetched = fetched.reshape(slab, stored, side, width)
    blocks = near_blocks.reshape(slab, stored, side, side)
    near = jnp.einsum("bkrc,bkcd->brd", blocks, fetched, preferred_element_type=jnp.float32)
    force_rows = force_rows.astype(jnp.bfloat16).reshape(slots, side, width)
    contrib = jnp.einsum("mcj,mjd->mcd", weights, force_rows, preferred_element_type=jnp.float32)
    rowhot = (
        (marker_rows[None, :] == jnp.arange(slab, dtype=jnp.int32)[:, None]) & mlive[None, :]
    ).astype(jnp.float32)
    spread = jnp.dot(rowhot, contrib.reshape(slots, side * width), precision=HP).reshape(
        slab, side, width
    )
    image = (near + spread).reshape(slab * side, width)
    gram = lax.psum(jnp.dot(image.T, image, precision=HP), ("row", "reach"))
    return image, gram


def solution(mesh):
    rows, reach = mesh.shape["row"], mesh.shape["reach"]
    devices = rows * reach
    paired = reach == 4 and rows % 2 == 0 and NG % devices == 0 and NG // devices >= 2

    def local(*args):
        if paired:
            image, gram = image_and_gram(rows, reach, *args)
        else:
            image, gram = plain_image_and_gram(*args)
        return factor(image, gram, image.shape[0] * devices)

    return jax.shard_map(
        local,
        mesh=mesh,
        in_specs=(
            P(("row", "reach"), None),
            P(("row", "reach"), None),
            P(("row", "reach")),
            P(("row", "reach"), None, None),
            P(("row", "reach")),
            P(("row", "reach")),
            P(("row", "reach")),
            P(("row", "reach"), None),
            P(),
        ),
        out_specs=(P(("row", "reach"), None), P()),
        check_vma=False,
    )
```

time: 332 us -> 74.9 us (0.23)
  waiting for transfers between devices: 255 us -> 0 us
  Pallas kernels: 0 us -> 52.3 us
  other arithmetic: 29.1 us -> 1.37 us
  between operations: 16.3 us -> 1.36 us
  matrix products: 12.5 us -> 0 us
    psum x2 -> x0, waiting for transfers between devices: 254 us -> none  [the longest x1 138 us: local(): totals = lax.psum(local_sums, ('row', 'reach'))]
    pallas_call x0 -> x2, Pallas kernels: none -> 52.3 us  [the longest x1 40.1 us: image_and_gram(): pl.pallas_call(functools.partial(image_kernel, rows, reach), out_shape=(j...]
    another operation x4 -> x0, other arithmetic: 22.2 us -> none  [the longest x3 12.4 us: local(): lower = jnp.linalg.cholesky(gram)]
    reshape x4 -> x6, local copies, waits for them, and re-layouts: 8.38 us -> 19.3 us  [the longest x2 13.7 us: image_and_gram(): near_blocks.reshape(slab, stored, side, side).transpose(0, 2, 1, 3)]
    dot_general x7 -> x0, matrix products: 10.5 us -> none  [the longest x1 4.61 us: local(): jnp.einsum('bkrc,bkcd->brd', blocks, fetched, preferred_element_type=jnp....]
    gather x2 -> x0, local copies, waits for them, and re-layouts: 6.17 us -> none  [the longest x1 4.53 us: local(): group_basis[near_cols]]
  transfers between devices with their start and end apart: 3 -> 0, of which waited for: 2 -> 0; matrix products, arithmetic and copies ran while one was open for 4% -> 0% of each run, Pallas kernels for 0% -> 0%
where the time goes in v1:
time: 74.9 us; the launch traced here: 74.5 us
  Pallas kernels  52.3 us (70%)
  local copies, waits for them, and re-layouts  19.5 us (26%)
  other arithmetic  1.37 us (2%)
  between operations  1.36 us (2%)
    pallas_call x1, Pallas kernels, image_and_gram(): pl.pallas_call(functools.partial(image_kernel, rows, reach), out_shape=(j...  40.1 us
    reshape x2, local copies, waits for them, and re-layouts, image_and_gram(): near_blocks.reshape(slab, stored, side, side).transpose(0, 2, 1, 3)  13.7 us
    pallas_call x1, Pallas kernels, factor(): pl.pallas_call(functools.partial(factor_kernel, float(total_rows) ** 0.5)...  12.2 us
    reshape x1, local copies, waits for them, and re-layouts, image_and_gram(): blocks = near_blocks.reshape(slab, stored, side, side).transpose(0, 2, 1,...  5.26 us

profile of v1, /device:TPU:0, one launch (start us, length us, event | category | flops | bytes accessed | tf_op | source)
XLA Modules:
  0.0 74.5 jit_solution(7197000058622165692)
XLA Ops:
  0.6 0.7 fusion
  1.3 0.1 copy.12
  1.4 0.1 reshape.26.cols
  2.2 0.7 compare_select_fusion.2.code
  2.8 6.3 %reshape.28 = bf16[32,7,64,64]{3,2,0,1:T(8,128)(2,1)} reshape(bf16[32,7,4096]{2,0,1:T(8,128)(2,1)} %param.12) | data formatting | bytes 3670016 | tf_op jit(solution)/shard_map/reshape | solution.py:231
  9.1 7.4 %copy.16 = bf16[32,7,64,64]{3,1,2,0:T(8,128)(2,1)} copy(bf16[32,7,64,64]{3,2,0,1:T(8,128)(2,1)} %reshape.28) | data formatting | bytes 3670016 | tf_op jit(solution)/shard_map/reshape | solution.py:231
  16.5 0.0 copy-start.2
  16.5 0.0 copy-start.3
  16.5 0.0 copy-start
  16.5 0.0 copy-start.1
  16.5 5.3 %reshape.29.blocks = bf16[32,64,448]{2,1,0:T(8,128)(2,1)S(1)} reshape(bf16[32,64,7,64]{3,2,1,0:T(8,128)(2,1)} %bitcast.13) | data formatting | bytes 3670016 | tf_op jit(solution)/shard_map/reshape | solution.py:233
  21.8 0.0 copy-done.2
  21.8 0.2 reshape.30.weights
  22.0 0.0 copy-done.3
  22.0 0.1 reshape.31
  22.1 0.1 copy.14.stiff
  22.2 0.0 copy-done
  22.3 0.0 copy-done.1
  22.3 40.1 %shard_map.104 = (f32[2048,128]{1,0:T(8,128)S(1)}, f32[4,32,128]{2,1,0:T(8,128)S(1)}) custom-call(s32[224]{0:T(256)S(1)} %reshape.26.cols, s32[16]{0:T(128)S(1)} %copy-done.1, s32[16]{0:T(128)S(1)} %compare_select_fusion.2.code, bf16[32,64,128]{2,1,0:T(8,128)(2,1)S(1)} %bitcast.11, bf16[32,64,448]{2,1,0:T(8,128)(2,1)S(1)} %reshape.29.blocks, ...), custom_call_target="tpu_custom_call" | custom-call | tf_op jit(solution)/shard_map/pallas_call | solution.py:243
  62.4 12.2 %shard_map.105 = (f32[2048,128]{1,0:T(8,128)}, f32[128,128]{1,0:T(8,128)}) custom-call(f32[2048,128]{1,0:T(8,128)S(1)} %get-tuple-element.4.image, f32[128,128]{1,0:T(8,128)S(1)} %bitcast.12), custom_call_target="tpu_custom_call" | custom-call | tf_op jit(solution)/shard_map/pallas_call | solution.py:338
  (2 shorter events, 0.0 us)
Async XLA Ops:
  16.5 5.3 %copy-start.2 = (bf16[16,4096]{1,0:T(8,128)(2,1)S(1)}, bf16[16,4096]{1,0:T(8,128)(2,1)}, u32[]{:S(2)}) copy-start(bf16[16,4096]{1,0:T(8,128)(2,1)} %param.16) | copy-start | bytes 393220
  16.5 5.5 %copy-start.3 = (f32[4096]{0:T(1024)S(1)}, f32[4096]{0:T(1024)}, u32[]{:S(2)}) copy-start(f32[4096]{0:T(1024)} %param.17) | copy-start | bytes 49156
  16.5 5.8 %copy-start = (bf16[2048,128]{1,0:T(8,128)(2,1)S(1)}, bf16[2048,128]{1,0:T(8,128)(2,1)}, u32[]{:S(2)}) copy-start(bf16[2048,128]{1,0:T(8,128)(2,1)} %param.9) | copy-start | bytes 1572868
  16.5 5.8 %copy-start.1 = (s32[16]{0:T(128)S(1)}, s32[16]{0:T(128)}, u32[]{:S(2)}) copy-start(s32[16]{0:T(128)} %mrow.1) | copy-start | bytes 196

commit v2 on v1

--- a/solution.py
+++ b/solution.py
@@ -62,7 +62,7 @@
     z = lax.axis_index("row")
     r = lax.axis_index("reach")
     slab, side, width = basis.shape
-    stored = blocks.shape[2] // side
+    stored = blocks.shape[1]
     slots = weights.shape[0]
     core = lax.rem(r, 2)
     sib = r + 1 - 2 * core
@@ -145,8 +145,9 @@
         fwd[c].wait()
 
     def near_step(i, carry):
-        fetched = jnp.concatenate([grp[cols[i * stored + k]] for k in range(stored)], axis=0)
-        acc = dot(blocks[i], fetched, 1, 0)
+        acc = dot(blocks[i, 0], grp[cols[i * stored]], 1, 0)
+        for k in range(1, stored):
+            acc = acc + dot(blocks[i, k], grp[cols[i * stored + k]], 1, 0)
         for m in range(slots):
             hit = jnp.where((mrow[m] == i) & (code[m] < 3), 1.0, 0.0)
             acc = acc + hit * contrib[m]
@@ -227,11 +228,7 @@
         marker_groups == base, 0, jnp.where(marker_groups == away, 1, 2)
     ).astype(jnp.int32)
     code = jnp.where(mlive, code, 3)
-    blocks = (
-        near_blocks.reshape(slab, stored, side, side)
-        .transpose(0, 2, 1, 3)
-        .reshape(slab, side, stored * side)
-    )
+    blocks = near_blocks.reshape(slab, stored, side, side)
     weights = marker_weights.reshape(slots, side, side)
     st = stiffness.reshape(NG, side)
     stiff = jnp.stack(

time: 74.9 us -> 69 us (0.921)
  local copies, waits for them, and re-layouts: 19.5 us -> 13.8 us
    reshape x3 -> x2, local copies, waits for them, and re-layouts: 18.9 us -> 11.1 us  [image_and_gram(): blocks = near_blocks.reshape(slab, stored, side, side)]
    unnamed x8 -> x10, local copies, waits for them, and re-layouts: 0.01 us -> 2.05 us
where the time goes in v2:
time: 69 us; the launch traced here: 68.7 us
  Pallas kernels  52.2 us (76%)
  local copies, waits for them, and re-layouts  13.8 us (20%)
  other arithmetic  1.37 us (2%)
  between operations  1.35 us (2%)
    pallas_call x1, Pallas kernels, image_and_gram(): pl.pallas_call(functools.partial(image_kernel, rows, reach), out_shape=(j...  40.1 us
    pallas_call x1, Pallas kernels, factor(): pl.pallas_call(functools.partial(factor_kernel, float(total_rows) ** 0.5)...  12.2 us
    reshape x2, local copies, waits for them, and re-layouts, image_and_gram(): blocks = near_blocks.reshape(slab, stored, side, side)  11.1 us
    unnamed x10, local copies, waits for them, and re-layouts  2.05 us

profile of v2, /device:TPU:0, one launch (start us, length us, event | category | flops | bytes accessed | tf_op | source)
XLA Modules:
  0.0 68.7 jit_solution(530449424496759674)
XLA Ops:
  0.6 0.7 %fusion = s32[32,7]{0,1:T(8,128)S(1)} fusion(s32[32,7]{0,1:T(8,128)} %param.10, s32[32]{0:T(128)} %param.11), kind=kLoop, calls=%fused_computation.1 | loop fusion | flops 448 | bytes 1920 | tf_op jit(solution)/shard_map/jit(_where)/select_n | solution.py:225
  1.3 0.1 copy.12
  1.4 0.1 reshape.23.cols
  2.2 0.7 compare_select_fusion.2.code
  2.8 6.3 %reshape.25 = bf16[32,7,64,64]{3,2,0,1:T(8,128)(2,1)} reshape(bf16[32,7,4096]{2,0,1:T(8,128)(2,1)} %param.12) | data formatting | bytes 3670016 | tf_op jit(solution)/shard_map/reshape | solution.py:231
  9.1 0.0 copy-start.3
  9.1 0.0 copy-start.4
  9.1 0.0 copy-start.1
  9.1 0.0 copy-start.2
  9.2 4.8 %copy.13.blocks = bf16[32,7,64,64]{3,2,1,0:T(8,128)(2,1)} copy(bf16[32,7,64,64]{3,2,0,1:T(8,128)(2,1)} %reshape.25) | data formatting | bytes 3670016 | tf_op jit(solution)/shard_map/reshape | solution.py:231
  13.9 0.0 copy-done.3
  13.9 0.2 reshape.26.weights
  14.2 0.0 copy-done.4
  14.2 0.1 reshape.27
  14.3 0.1 copy.14.stiff
  14.4 0.0 copy-done.1
  14.4 0.0 copy-done.2
  14.4 0.0 copy-start
  14.4 2.0 %copy-done = bf16[32,7,64,64]{3,2,1,0:T(8,128)(2,1)S(1)} copy-done((bf16[32,7,64,64]{3,2,1,0:T(8,128)(2,1)S(1)}, bf16[32,7,64,64]{3,2,1,0:T(8,128)(2,1)}, u32[]{:S(2)}) %copy-start) | copy-done | bytes 1835032
  16.5 40.1 %shard_map.104 = (f32[2048,128]{1,0:T(8,128)S(1)}, f32[4,32,128]{2,1,0:T(8,128)S(1)}) custom-call(s32[224]{0:T(256)S(1)} %reshape.23.cols, s32[16]{0:T(128)S(1)} %copy-done.2, s32[16]{0:T(128)S(1)} %compare_select_fusion.2.code, bf16[32,64,128]{2,1,0:T(8,128)(2,1)S(1)} %bitcast.8, bf16[32,7,64,64]{3,2,1,0:T(8,128)(2,1)S(1)} %copy-done, ...), custom_call_target="tpu_custom_call" | custom-call | tf_op jit(solution)/shard_map/pallas_call | solution.py:240
  56.6 12.2 %shard_map.105 = (f32[2048,128]{1,0:T(8,128)}, f32[128,128]{1,0:T(8,128)}) custom-call(f32[2048,128]{1,0:T(8,128)S(1)} %get-tuple-element.4.image, f32[128,128]{1,0:T(8,128)S(1)} %bitcast.9), custom_call_target="tpu_custom_call" | custom-call | tf_op jit(solution)/shard_map/pallas_call | solution.py:335
  (2 shorter events, 0.0 us)
Async XLA Ops:
  9.1 4.8 %copy-start.3 = (bf16[16,4096]{1,0:T(8,128)(2,1)S(1)}, bf16[16,4096]{1,0:T(8,128)(2,1)}, u32[]{:S(2)}) copy-start(bf16[16,4096]{1,0:T(8,128)(2,1)} %param.16) | copy-start | bytes 393220
  9.1 5.1 %copy-start.4 = (f32[4096]{0:T(1024)S(1)}, f32[4096]{0:T(1024)}, u32[]{:S(2)}) copy-start(f32[4096]{0:T(1024)} %param.17) | copy-start | bytes 49156
  9.1 5.3 %copy-start.1 = (bf16[2048,128]{1,0:T(8,128)(2,1)S(1)}, bf16[2048,128]{1,0:T(8,128)(2,1)}, u32[]{:S(2)}) copy-start(bf16[2048,128]{1,0:T(8,128)(2,1)} %param.9) | copy-start | bytes 1572868
  9.1 5.3 %copy-start.2 = (s32[16]{0:T(128)S(1)}, s32[16]{0:T(128)}, u32[]{:S(2)}) copy-start(s32[16]{0:T(128)} %mrow.1) | copy-start | bytes 196
  14.4 2.0 %copy-start = (bf16[32,7,64,64]{3,2,1,0:T(8,128)(2,1)S(1)}, bf16[32,7,64,64]{3,2,1,0:T(8,128)(2,1)}, u32[]{:S(2)}) copy-start(bf16[32,7,64,64]{3,2,1,0:T(8,128)(2,1)} %copy.13.blocks) | copy-start | bytes 5505028

commit v3 on v2

--- a/solution.py
+++ b/solution.py
@@ -138,6 +138,16 @@
 
     lax.fori_loop(0, slots, spread_step, 0)
 
+    def own_step(i, carry):
+        acc = dot(blocks[i, 0], basis[i], 1, 0)
+        for m in range(slots):
+            hit = jnp.where((mrow[m] == i) & (code[m] < 3), 1.0, 0.0)
+            acc = acc + hit * contrib[m]
+        image[pl.ds(pl.multiple_of(i * side, side), side)] = acc
+        return carry
+
+    lax.fori_loop(0, slab, own_step, 0)
+
     own.wait()
     to_sib.wait()
     for c in range(CHUNKS):
@@ -145,13 +155,11 @@
         fwd[c].wait()
 
     def near_step(i, carry):
-        acc = dot(blocks[i, 0], grp[cols[i * stored]], 1, 0)
+        at = pl.ds(pl.multiple_of(i * side, side), side)
+        acc = image[at]
         for k in range(1, stored):
             acc = acc + dot(blocks[i, k], grp[cols[i * stored + k]], 1, 0)
-        for m in range(slots):
-            hit = jnp.where((mrow[m] == i) & (code[m] < 3), 1.0, 0.0)
-            acc = acc + hit * contrib[m]
-        image[pl.ds(pl.multiple_of(i * side, side), side)] = acc
+        image[at] = acc
         return carry
 
     lax.fori_loop(0, slab, near_step, 0)

time: 69 us -> 72.9 us (1.057)
  Pallas kernels: 52.2 us -> 56.1 us
    pallas_call x1, Pallas kernels: 40.1 us -> 43.9 us  [image_and_gram(): pl.pallas_call(functools.partial(image_kernel, rows, reach), out_shape=(j...]
where the time goes in v3:
time: 72.9 us; the launch traced here: 72.6 us
  Pallas kernels  56.1 us (77%)
  local copies, waits for them, and re-layouts  13.8 us (19%)
  other arithmetic  1.37 us (2%)
  between operations  1.35 us (2%)
    pallas_call x1, Pallas kernels, image_and_gram(): pl.pallas_call(functools.partial(image_kernel, rows, reach), out_shape=(j...  43.9 us
    pallas_call x1, Pallas kernels, factor(): pl.pallas_call(functools.partial(factor_kernel, float(total_rows) ** 0.5)...  12.2 us
    reshape x2, local copies, waits for them, and re-layouts, image_and_gram(): blocks = near_blocks.reshape(slab, stored, side, side)  11.1 us
    unnamed x10, local copies, waits for them, and re-layouts  2.05 us

profile of v3, /device:TPU:0, one launch (start us, length us, event | category | flops | bytes accessed | tf_op | source)
XLA Modules:
  0.0 72.6 jit_solution(2520946348097569565)
XLA Ops:
  0.6 0.7 fusion
  1.3 0.1 copy.12
  1.4 0.1 reshape.23.cols
  2.2 0.7 compare_select_fusion.2.code
  2.8 6.3 %reshape.25 = bf16[32,7,64,64]{3,2,0,1:T(8,128)(2,1)} reshape(bf16[32,7,4096]{2,0,1:T(8,128)(2,1)} %param.12) | data formatting | bytes 3670016 | tf_op jit(solution)/shard_map/reshape | solution.py:239
  9.1 0.0 copy-start.3
  9.1 0.0 copy-start.4
  9.1 0.0 copy-start.1
  9.1 0.0 copy-start.2
  9.2 4.8 %copy.13.blocks = bf16[32,7,64,64]{3,2,1,0:T(8,128)(2,1)} copy(bf16[32,7,64,64]{3,2,0,1:T(8,128)(2,1)} %reshape.25) | data formatting | bytes 3670016 | tf_op jit(solution)/shard_map/reshape | solution.py:239
  13.9 0.0 copy-done.3
  13.9 0.2 reshape.26.weights
  14.2 0.0 copy-done.4
  14.2 0.1 reshape.27
  14.3 0.1 copy.14.stiff
  14.4 0.0 copy-done.1
  14.4 0.0 copy-done.2
  14.4 0.0 copy-start
  14.4 2.0 %copy-done = bf16[32,7,64,64]{3,2,1,0:T(8,128)(2,1)S(1)} copy-done((bf16[32,7,64,64]{3,2,1,0:T(8,128)(2,1)S(1)}, bf16[32,7,64,64]{3,2,1,0:T(8,128)(2,1)}, u32[]{:S(2)}) %copy-start) | copy-done | bytes 1835032
  16.5 43.9 %shard_map.104 = (f32[2048,128]{1,0:T(8,128)S(1)}, f32[4,32,128]{2,1,0:T(8,128)S(1)}) custom-call(s32[224]{0:T(256)S(1)} %reshape.23.cols, s32[16]{0:T(128)S(1)} %copy-done.2, s32[16]{0:T(128)S(1)} %compare_select_fusion.2.code, bf16[32,64,128]{2,1,0:T(8,128)(2,1)S(1)} %bitcast.8, bf16[32,7,64,64]{3,2,1,0:T(8,128)(2,1)S(1)} %copy-done, ...), custom_call_target="tpu_custom_call" | custom-call | tf_op jit(solution)/shard_map/pallas_call | solution.py:248
  60.4 12.2 %shard_map.105 = (f32[2048,128]{1,0:T(8,128)}, f32[128,128]{1,0:T(8,128)}) custom-call(f32[2048,128]{1,0:T(8,128)S(1)} %get-tuple-element.4.image, f32[128,128]{1,0:T(8,128)S(1)} %bitcast.9), custom_call_target="tpu_custom_call" | custom-call | tf_op jit(solution)/shard_map/pallas_call | solution.py:343
  (2 shorter events, 0.0 us)
Async XLA Ops:
  9.1 4.8 %copy-start.3 = (bf16[16,4096]{1,0:T(8,128)(2,1)S(1)}, bf16[16,4096]{1,0:T(8,128)(2,1)}, u32[]{:S(2)}) copy-start(bf16[16,4096]{1,0:T(8,128)(2,1)} %param.16) | copy-start | bytes 393220
  9.1 5.1 %copy-start.4 = (f32[4096]{0:T(1024)S(1)}, f32[4096]{0:T(1024)}, u32[]{:S(2)}) copy-start(f32[4096]{0:T(1024)} %param.17) | copy-start | bytes 49156
  9.1 5.3 %copy-start.1 = (bf16[2048,128]{1,0:T(8,128)(2,1)S(1)}, bf16[2048,128]{1,0:T(8,128)(2,1)}, u32[]{:S(2)}) copy-start(bf16[2048,128]{1,0:T(8,128)(2,1)} %param.9) | copy-start | bytes 1572868
  9.1 5.3 %copy-start.2 = (s32[16]{0:T(128)S(1)}, s32[16]{0:T(128)}, u32[]{:S(2)}) copy-start(s32[16]{0:T(128)} %mrow.1) | copy-start | bytes 196
  14.4 2.0 %copy-start = (bf16[32,7,64,64]{3,2,1,0:T(8,128)(2,1)S(1)}, bf16[32,7,64,64]{3,2,1,0:T(8,128)(2,1)}, u32[]{:S(2)}) copy-start(bf16[32,7,64,64]{3,2,1,0:T(8,128)(2,1)} %copy.13.blocks) | copy-start | bytes 5505028

commit v4 on v2

--- a/solution.py
+++ b/solution.py
@@ -10,6 +10,7 @@
 BS = 64
 NG = 64
 CHUNKS = 4
+TOGETHER = 4
 HP = lax.Precision.HIGHEST
 MESH = pl.DeviceIdType.MESH
 VM = pl.BlockSpec(memory_space=pltpu.VMEM)
@@ -104,13 +105,17 @@
 
     sums[...] = jnp.zeros_like(sums)
 
-    def gather_step(m, carry):
-        value = dot(weights[m], basis[mrow[m]], 0, 0)
+    def gather_step(t, carry):
+        ms = [t * TOGETHER + u for u in range(TOGETHER)]
+        values = [dot(weights[m], basis[mrow[m]], 0, 0) for m in ms]
         for g in range(3):
-            sums[g] = sums[g] + jnp.where(code[m] == g, 1.0, 0.0) * value
+            total = sums[g]
+            for m, value in zip(ms, values):
+                total = total + jnp.where(code[m] == g, 1.0, 0.0) * value
+            sums[g] = total
         return carry
 
-    lax.fori_loop(0, slots, gather_step, 0)
+    lax.fori_loop(0, slots // TOGETHER, gather_step, 0)
     swap = remote(
         sums.at[pl.ds(0, 2)], other, m_send, m_recv, (lax.rem(z + rows // 2, rows), r)
     )
@@ -132,11 +137,14 @@
     force[0] = force_of(sums[0] + other[1], 0)
     force[1] = force_of(sums[1] + other[0], 1)
 
-    def spread_step(m, carry):
-        contrib[m] = dot(weights[m], force[jnp.minimum(code[m], 2)], 1, 0)
+    def spread_step(t, carry):
+        ms = [t * TOGETHER + u for u in range(TOGETHER)]
+        values = [dot(weights[m], force[jnp.minimum(code[m], 2)], 1, 0) for m in ms]
+        for m, value in zip(ms, values):
+            contrib[m] = value
         return carry
 
-    lax.fori_loop(0, slots, spread_step, 0)
+    lax.fori_loop(0, slots // TOGETHER, spread_step, 0)
 
     own.wait()
     to_sib.wait()
@@ -144,17 +152,25 @@
         to_far[c].wait_send()
         fwd[c].wait()
 
-    def near_step(i, carry):
-        acc = dot(blocks[i, 0], grp[cols[i * stored]], 1, 0)
+    def near_step(t, carry):
+        lines = [t * TOGETHER + u for u in range(TOGETHER)]
+        accs = [dot(blocks[i, 0], grp[cols[i * stored]], 1, 0) for i in lines]
         for k in range(1, stored):
-            acc = acc + dot(blocks[i, k], grp[cols[i * stored + k]], 1, 0)
+            accs = [
+                acc + dot(blocks[i, k], grp[cols[i * stored + k]], 1, 0)
+                for i, acc in zip(lines, accs)
+            ]
         for m in range(slots):
-            hit = jnp.where((mrow[m] == i) & (code[m] < 3), 1.0, 0.0)
-            acc = acc + hit * contrib[m]
-        image[pl.ds(pl.multiple_of(i * side, side), side)] = acc
+            term = contrib[m]
+            accs = [
+                acc + jnp.where((mrow[m] == i) & (code[m] < 3), 1.0, 0.0) * term
+                for i, acc in zip(lines, accs)
+            ]
+        for i, acc in zip(lines, accs):
+            image[pl.ds(pl.multiple_of(i * side, side), side)] = acc
         return carry
 
-    lax.fori_loop(0, slab, near_step, 0)
+    lax.fori_loop(0, slab // TOGETHER, near_step, 0)
 
     part[...] = jnp.zeros_like(part)
 

time: 69 us -> 64.8 us (0.939)
  Pallas kernels: 52.2 us -> 48 us
    pallas_call x1, Pallas kernels: 40.1 us -> 35.9 us  [image_and_gram(): pl.pallas_call(functools.partial(image_kernel, rows, reach), out_shape=(j...]
where the time goes in v4:
time: 64.8 us; the launch traced here: 64.5 us
  Pallas kernels  48 us (74%)
  local copies, waits for them, and re-layouts  13.8 us (21%)
  other arithmetic  1.37 us (2%)
  between operations  1.35 us (2%)
    pallas_call x1, Pallas kernels, image_and_gram(): pl.pallas_call(functools.partial(image_kernel, rows, reach), out_shape=(j...  35.9 us
    pallas_call x1, Pallas kernels, factor(): pl.pallas_call(functools.partial(factor_kernel, float(total_rows) ** 0.5)...  12.2 us
    reshape x2, local copies, waits for them, and re-layouts, image_and_gram(): blocks = near_blocks.reshape(slab, stored, side, side)  11.1 us
    unnamed x10, local copies, waits for them, and re-layouts  2.05 us

profile of v4, /device:TPU:0, one launch (start us, length us, event | category | flops | bytes accessed | tf_op | source)
XLA Modules:
  0.0 64.5 jit_solution(1411635107271584066)
XLA Ops:
  0.6 0.7 %fusion = s32[32,7]{0,1:T(8,128)S(1)} fusion(s32[32,7]{0,1:T(8,128)} %param.10, s32[32]{0:T(128)} %param.11), kind=kLoop, calls=%fused_computation.1 | loop fusion | flops 448 | bytes 1920 | tf_op jit(solution)/shard_map/jit(_where)/select_n | solution.py:241
  1.3 0.1 copy.12
  1.4 0.1 reshape.23.cols
  2.2 0.7 %compare_select_fusion.2.code = s32[16]{0:T(128)S(1)} fusion(s32[16]{0:T(128)} %param.14, s32[]{:T(128)S(6)} %rem.18, s32[]{:T(128)S(6)} %mul.7, s32[]{:T(128)} %bitcast.7), kind=kLoop, calls=%fused_computation.5 | loop fusion | flops 96 | bytes 140 | tf_op jit(solution)/shard_map/jit(_where)/select_n | solution.py:246
  2.8 6.3 %reshape.25 = bf16[32,7,64,64]{3,2,0,1:T(8,128)(2,1)} reshape(bf16[32,7,4096]{2,0,1:T(8,128)(2,1)} %param.12) | data formatting | bytes 3670016 | tf_op jit(solution)/shard_map/reshape | solution.py:247
  9.1 0.0 copy-start.3
  9.1 0.0 copy-start.4
  9.1 0.0 copy-start.1
  9.1 0.0 copy-start.2
  9.2 4.8 %copy.13.blocks = bf16[32,7,64,64]{3,2,1,0:T(8,128)(2,1)} copy(bf16[32,7,64,64]{3,2,0,1:T(8,128)(2,1)} %reshape.25) | data formatting | bytes 3670016 | tf_op jit(solution)/shard_map/reshape | solution.py:247
  13.9 0.0 copy-done.3
  13.9 0.2 reshape.26.weights
  14.2 0.0 copy-done.4
  14.2 0.1 reshape.27
  14.3 0.1 copy.14.stiff
  14.4 0.0 copy-done.1
  14.4 0.0 copy-done.2
  14.4 0.0 copy-start
  14.4 2.0 %copy-done = bf16[32,7,64,64]{3,2,1,0:T(8,128)(2,1)S(1)} copy-done((bf16[32,7,64,64]{3,2,1,0:T(8,128)(2,1)S(1)}, bf16[32,7,64,64]{3,2,1,0:T(8,128)(2,1)}, u32[]{:S(2)}) %copy-start) | copy-done | bytes 1835032
  16.5 35.9 %shard_map.104 = (f32[2048,128]{1,0:T(8,128)S(1)}, f32[4,32,128]{2,1,0:T(8,128)S(1)}) custom-call(s32[224]{0:T(256)S(1)} %reshape.23.cols, s32[16]{0:T(128)S(1)} %copy-done.2, s32[16]{0:T(128)S(1)} %compare_select_fusion.2.code, bf16[32,64,128]{2,1,0:T(8,128)(2,1)S(1)} %bitcast.8, bf16[32,7,64,64]{3,2,1,0:T(8,128)(2,1)S(1)} %copy-done, ...), custom_call_target="tpu_custom_call" | custom-call | tf_op jit(solution)/shard_map/pallas_call | solution.py:256
  52.4 12.2 %shard_map.105 = (f32[2048,128]{1,0:T(8,128)}, f32[128,128]{1,0:T(8,128)}) custom-call(f32[2048,128]{1,0:T(8,128)S(1)} %get-tuple-element.4.image, f32[128,128]{1,0:T(8,128)S(1)} %bitcast.9), custom_call_target="tpu_custom_call" | custom-call | tf_op jit(solution)/shard_map/pallas_call | solution.py:351
  (2 shorter events, 0.0 us)
Async XLA Ops:
  9.1 4.8 %copy-start.3 = (bf16[16,4096]{1,0:T(8,128)(2,1)S(1)}, bf16[16,4096]{1,0:T(8,128)(2,1)}, u32[]{:S(2)}) copy-start(bf16[16,4096]{1,0:T(8,128)(2,1)} %param.16) | copy-start | bytes 393220
  9.1 5.1 %copy-start.4 = (f32[4096]{0:T(1024)S(1)}, f32[4096]{0:T(1024)}, u32[]{:S(2)}) copy-start(f32[4096]{0:T(1024)} %param.17) | copy-start | bytes 49156
  9.1 5.3 %copy-start.1 = (bf16[2048,128]{1,0:T(8,128)(2,1)S(1)}, bf16[2048,128]{1,0:T(8,128)(2,1)}, u32[]{:S(2)}) copy-start(bf16[2048,128]{1,0:T(8,128)(2,1)} %param.9) | copy-start | bytes 1572868
  9.1 5.3 %copy-start.2 = (s32[16]{0:T(128)S(1)}, s32[16]{0:T(128)}, u32[]{:S(2)}) copy-start(s32[16]{0:T(128)} %mrow.1) | copy-start | bytes 196
  14.4 2.0 %copy-start = (bf16[32,7,64,64]{3,2,1,0:T(8,128)(2,1)S(1)}, bf16[32,7,64,64]{3,2,1,0:T(8,128)(2,1)}, u32[]{:S(2)}) copy-start(bf16[32,7,64,64]{3,2,1,0:T(8,128)(2,1)} %copy.13.blocks) | copy-start | bytes 5505028

commit v5 on v4

--- a/solution.py
+++ b/solution.py
@@ -35,6 +35,8 @@
     stiff,
     image,
     gram,
+    held,
+    held_sem,
     grp,
     sums,
     other,
@@ -63,7 +65,7 @@
     z = lax.axis_index("row")
     r = lax.axis_index("reach")
     slab, side, width = basis.shape
-    stored = blocks.shape[1]
+    stored = blocks.shape[0]
     slots = weights.shape[0]
     core = lax.rem(r, 2)
     sib = r + 1 - 2 * core
@@ -101,6 +103,8 @@
     to_sib.start()
     own = pltpu.make_async_copy(basis, grp.at[pl.ds(r * slab, slab)], local_sem)
     own.start()
+    load = pltpu.make_async_copy(blocks, held, held_sem)
+    load.start()
     grp[reach * slab] = jnp.zeros((side, width), grp.dtype)
 
     sums[...] = jnp.zeros_like(sums)
@@ -147,6 +151,7 @@
     lax.fori_loop(0, slots // TOGETHER, spread_step, 0)
 
     own.wait()
+    load.wait()
     to_sib.wait()
     for c in range(CHUNKS):
         to_far[c].wait_send()
@@ -154,10 +159,10 @@
 
     def near_step(t, carry):
         lines = [t * TOGETHER + u for u in range(TOGETHER)]
-        accs = [dot(blocks[i, 0], grp[cols[i * stored]], 1, 0) for i in lines]
+        accs = [dot(held[0, i], grp[cols[i * stored]], 1, 0) for i in lines]
         for k in range(1, stored):
             accs = [
-                acc + dot(blocks[i, k], grp[cols[i * stored + k]], 1, 0)
+                acc + dot(held[k, i], grp[cols[i * stored + k]], 1, 0)
                 for i, acc in zip(lines, accs)
             ]
         for m in range(slots):
@@ -244,7 +249,7 @@
         marker_groups == base, 0, jnp.where(marker_groups == away, 1, 2)
     ).astype(jnp.int32)
     code = jnp.where(mlive, code, 3)
-    blocks = near_blocks.reshape(slab, stored, side, side)
+    blocks = near_blocks.reshape(slab, stored, side, side).transpose(1, 0, 2, 3)
     weights = marker_weights.reshape(slots, side, side)
     st = stiffness.reshape(NG, side)
     stiff = jnp.stack(
@@ -259,9 +264,11 @@
             jax.ShapeDtypeStruct((slab * side, width), f32),
             jax.ShapeDtypeStruct((reach, q, width), f32),
         ),
-        in_specs=[SM, SM, SM, VM, VM, VM, VM],
+        in_specs=[SM, SM, SM, VM, pl.BlockSpec(memory_space=pl.ANY), VM, VM],
         out_specs=(VM, VM),
         scratch_shapes=[
+            pltpu.VMEM((stored, slab, side, side), bf16),
+            dma,
             pltpu.VMEM((reach * slab + 1, side, width), bf16),
             pltpu.VMEM((3, side, width), f32),
             pltpu.VMEM((2, side, width), f32),
@@ -288,7 +295,7 @@
             dma((reach - 1,)),
         ],
         compiler_params=pltpu.CompilerParams(
-            collective_id=0, has_side_effects=True, vmem_limit_bytes=40 * 1024 * 1024
+            collective_id=0, has_side_effects=True, vmem_limit_bytes=56 * 1024 * 1024
         ),
     )(
         cols,

time: 64.8 us -> 65.9 us (1.017)
  Pallas kernels: 48 us -> 49.6 us
  local copies, waits for them, and re-layouts: 13.8 us -> 12.6 us
    reshape x2 -> x1, local copies, waits for them, and re-layouts: 11.1 us -> 6.3 us  [image_and_gram(): blocks = near_blocks.reshape(slab, stored, side, side).transpose(1, 0, 2, 3)]
    reshape x1, local copies, waits for them, and re-layouts: 0.24 us -> 1.89 us  [image_and_gram(): weights = marker_weights.reshape(slots, side, side)]
    pallas_call x1, Pallas kernels: 35.9 us -> 37.5 us  [image_and_gram(): pl.pallas_call(functools.partial(image_kernel, rows, reach), out_shape=(j...]
    reshape x1, local copies, waits for them, and re-layouts: 0.07 us -> 0.79 us  [image_and_gram(): st = stiffness.reshape(NG, side)]
    unnamed x10 -> x4, local copies, waits for them, and re-layouts: 2.05 us -> 2.06 us
where the time goes in v5:
time: 65.9 us; the launch traced here: 65.4 us
  Pallas kernels  49.6 us (75%)
  local copies, waits for them, and re-layouts  12.6 us (19%)
  other arithmetic  1.9 us (3%)
  between operations  1.32 us (2%)
    pallas_call x1, Pallas kernels, image_and_gram(): pl.pallas_call(functools.partial(image_kernel, rows, reach), out_shape=(j...  37.5 us
    pallas_call x1, Pallas kernels, factor(): pl.pallas_call(functools.partial(factor_kernel, float(total_rows) ** 0.5)...  12.2 us
    reshape x1, local copies, waits for them, and re-layouts, image_and_gram(): blocks = near_blocks.reshape(slab, stored, side, side).transpose(1, 0, 2, 3)  6.3 us
    unnamed x4, local copies, waits for them, and re-layouts  2.06 us
    reshape x1, local copies, waits for them, and re-layouts, image_and_gram(): weights = marker_weights.reshape(slots, side, side)  1.89 us

profile of v5, /device:TPU:0, one launch (start us, length us, event | category | flops | bytes accessed | tf_op | source)
XLA Modules:
  0.0 65.4 jit_solution(5106422486676018403)
XLA Ops:
  1.3 1.2 %compare_select_fusion.2.code = s32[16]{0:T(128)} fusion(s32[16]{0:T(128)} %param.14, s32[]{:T(128)S(6)} %rem.18, s32[]{:T(128)S(6)} %mul.7, s32[]{:T(128)} %bitcast.8), kind=kLoop, calls=%fused_computation.5 | loop fusion | flops 96 | bytes 140 | tf_op jit(solution)/shard_map/jit(_where)/select_n | solution.py:251
  2.5 0.7 %fusion = s32[32,7]{0,1:T(8,128)S(1)} fusion(s32[32,7]{0,1:T(8,128)} %param.10, s32[32]{0:T(128)} %param.11), kind=kLoop, calls=%fused_computation.1 | loop fusion | flops 448 | bytes 1920 | tf_op jit(solution)/shard_map/jit(_where)/select_n | solution.py:246
  3.2 0.1 copy.11
  3.3 0.7 %reshape.23.cols = s32[224]{0:T(256)} reshape(s32[32,7]{1,0:T(8,128)S(1)} %copy.11) | data formatting | bytes 1792 | tf_op jit(solution)/shard_map/reshape | solution.py:246
  3.9 0.8 %reshape.27 = f32[64,64]{1,0:T(8,128)S(1)} reshape(f32[4096]{0:T(1024)} %param.17) | data formatting | bytes 32768 | tf_op jit(solution)/shard_map/reshape | solution.py:254
  4.8 0.8 %copy.12.stiff = f32[3,64,1]{2,1,0:T(8,128)} copy(f32[3,64,1]{1,0,2:T(4,128)S(1)} %maximum_bitcast_fusion) | data formatting | bytes 1536 | tf_op jit(solution)/shard_map/broadcast_in_dim | solution.py:255
  5.5 1.9 %reshape.26.weights = bf16[16,64,64]{2,1,0:T(8,128)(2,1)} reshape(bf16[16,4096]{1,0:T(8,128)(2,1)} %param.16) | data formatting | bytes 262144 | tf_op jit(solution)/shard_map/reshape | solution.py:253
  7.4 6.3 %reshape.25 = bf16[32,7,64,64]{3,2,0,1:T(8,128)(2,1)} reshape(bf16[32,7,4096]{2,0,1:T(8,128)(2,1)} %param.12) | data formatting | bytes 3670016 | tf_op jit(solution)/shard_map/reshape | solution.py:252
  13.7 37.5 %shard_map.104 = (f32[2048,128]{1,0:T(8,128)}, f32[4,32,128]{2,1,0:T(8,128)}) custom-call(s32[224]{0:T(256)} %reshape.23.cols, s32[16]{0:T(128)} %mrow.1, s32[16]{0:T(128)} %compare_select_fusion.2.code, bf16[32,64,128]{2,1,0:T(8,128)(2,1)} %bitcast.11, bf16[7,32,64,64]{3,2,1,0:T(8,128)(2,1)} %bitcast.10, bf16[16,64,64]{2,1,0:T(8,128)(2,1)} %reshape.26.weights, ...), custom_call_target="tpu_custom_call" | custom-call | tf_op jit(solution)/shard_map/pallas_call | solution.py:261
  51.2 0.0 copy-start
  51.2 1.2 %copy-done = f32[2048,128]{1,0:T(8,128)S(1)} copy-done((f32[2048,128]{1,0:T(8,128)S(1)}, f32[2048,128]{1,0:T(8,128)}, u32[]{:S(2)}) %copy-start) | copy-done | bytes 1048600
  52.4 0.0 copy-start.1
  52.4 0.8 %copy-done.1 = f32[4,32,128]{2,1,0:T(8,128)S(1)} copy-done((f32[4,32,128]{2,1,0:T(8,128)S(1)}, f32[4,32,128]{2,1,0:T(8,128)}, u32[]{:S(2)}) %copy-start.1) | copy-done | bytes 65560
  53.2 12.2 %shard_map.105 = (f32[2048,128]{1,0:T(8,128)}, f32[128,128]{1,0:T(8,128)}) custom-call(f32[2048,128]{1,0:T(8,128)S(1)} %copy-done, f32[128,128]{1,0:T(8,128)S(1)} %bitcast.9), custom_call_target="tpu_custom_call" | custom-call | tf_op jit(solution)/shard_map/pallas_call | solution.py:358
  (2 shorter events, 0.0 us)
Async XLA Ops:
  51.2 1.2 %copy-start = (f32[2048,128]{1,0:T(8,128)S(1)}, f32[2048,128]{1,0:T(8,128)}, u32[]{:S(2)}) copy-start(f32[2048,128]{1,0:T(8,128)} %get-tuple-element.4.image) | copy-start | bytes 3145732
  52.4 0.8 %copy-start.1 = (f32[4,32,128]{2,1,0:T(8,128)S(1)}, f32[4,32,128]{2,1,0:T(8,128)}, u32[]{:S(2)}) copy-start(f32[4,32,128]{2,1,0:T(8,128)} %get-tuple-element.5) | copy-start | bytes 196612

commit v6 on v5

--- a/solution.py
+++ b/solution.py
@@ -295,7 +295,7 @@
             dma((reach - 1,)),
         ],
         compiler_params=pltpu.CompilerParams(
-            collective_id=0, has_side_effects=True, vmem_limit_bytes=56 * 1024 * 1024
+            collective_id=0, has_side_effects=True, vmem_limit_bytes=40 * 1024 * 1024
         ),
     )(
         cols,

time: 65.9 us -> 61.8 us (0.938)
  local copies, waits for them, and re-layouts: 12.6 us -> 10.6 us
  Pallas kernels: 49.6 us -> 48.1 us
    pallas_call x1, Pallas kernels: 37.5 us -> 35.9 us  [image_and_gram(): pl.pallas_call(functools.partial(image_kernel, rows, reach), out_shape=(j...]
    reshape x1, local copies, waits for them, and re-layouts: 1.89 us -> 1.18 us  [image_and_gram(): weights = marker_weights.reshape(slots, side, side)]
    unnamed x4 -> x6, local copies, waits for them, and re-layouts: 2.06 us -> 2.04 us
where the time goes in v6:
time: 61.8 us; the launch traced here: 61.5 us
  Pallas kernels  48.1 us (78%)
  local copies, waits for them, and re-layouts  10.6 us (17%)
  between operations  1.39 us (2%)
  other arithmetic  1.36 us (2%)
    pallas_call x1, Pallas kernels, image_and_gram(): pl.pallas_call(functools.partial(image_kernel, rows, reach), out_shape=(j...  35.9 us
    pallas_call x1, Pallas kernels, factor(): pl.pallas_call(functools.partial(factor_kernel, float(total_rows) ** 0.5)...  12.2 us
    reshape x1, local copies, waits for them, and re-layouts, image_and_gram(): blocks = near_blocks.reshape(slab, stored, side, side).transpose(1, 0, 2, 3)  6.3 us
    unnamed x6, local copies, waits for them, and re-layouts  2.04 us

profile of v6, /device:TPU:0, one launch (start us, length us, event | category | flops | bytes accessed | tf_op | source)
XLA Modules:
  0.0 61.5 jit_solution(7563306952449807660)
XLA Ops:
  0.6 0.0 copy-start.2
  0.6 0.0 copy-start.1
  1.4 0.7 %compare_select_fusion.2.code = s32[16]{0:T(128)S(1)} fusion(s32[16]{0:T(128)} %param.14, s32[]{:T(128)S(6)} %rem.18, s32[]{:T(128)S(6)} %mul.7, s32[]{:T(128)} %bitcast.8), kind=kLoop, calls=%fused_computation.5 | loop fusion | flops 96 | bytes 140 | tf_op jit(solution)/shard_map/jit(_where)/select_n | solution.py:251
  2.0 0.7 %fusion = s32[32,7]{0,1:T(8,128)S(1)} fusion(s32[32,7]{0,1:T(8,128)} %param.10, s32[32]{0:T(128)} %param.11), kind=kLoop, calls=%fused_computation.1 | loop fusion | flops 448 | bytes 1920 | tf_op jit(solution)/shard_map/jit(_where)/select_n | solution.py:246
  2.7 0.1 copy.11
  2.8 0.1 reshape.23.cols
  2.9 0.8 %reshape.27 = f32[64,64]{1,0:T(8,128)S(1)} reshape(f32[4096]{0:T(1024)} %param.17) | data formatting | bytes 32768 | tf_op jit(solution)/shard_map/reshape | solution.py:254
  3.7 0.1 copy.12.stiff
  3.8 1.2 %reshape.26.weights = bf16[16,64,64]{2,1,0:T(8,128)(2,1)S(1)} reshape(bf16[16,4096]{1,0:T(8,128)(2,1)} %param.16) | data formatting | bytes 262144 | tf_op jit(solution)/shard_map/reshape | solution.py:253
  5.0 6.3 %reshape.25 = bf16[32,7,64,64]{3,2,0,1:T(8,128)(2,1)} reshape(bf16[32,7,4096]{2,0,1:T(8,128)(2,1)} %param.12) | data formatting | bytes 3670016 | tf_op jit(solution)/shard_map/reshape | solution.py:252
  11.3 0.0 copy-done.2
  11.3 0.0 copy-done.1
  11.3 0.0 copy-start
  11.3 2.0 %copy-done = bf16[32,7,64,64]{3,2,0,1:T(8,128)(2,1)S(1)} copy-done((bf16[32,7,64,64]{3,2,0,1:T(8,128)(2,1)S(1)}, bf16[32,7,64,64]{3,2,0,1:T(8,128)(2,1)}, u32[]{:S(2)}) %copy-start) | copy-done | bytes 1835032
  13.4 35.9 %shard_map.104 = (f32[2048,128]{1,0:T(8,128)S(1)}, f32[4,32,128]{2,1,0:T(8,128)S(1)}) custom-call(s32[224]{0:T(256)S(1)} %reshape.23.cols, s32[16]{0:T(128)S(1)} %copy-done.2, s32[16]{0:T(128)S(1)} %compare_select_fusion.2.code, bf16[32,64,128]{2,1,0:T(8,128)(2,1)S(1)} %bitcast.10, bf16[7,32,64,64]{3,2,1,0:T(8,128)(2,1)S(1)} %bitcast.9, ...), custom_call_target="tpu_custom_call" | custom-call | tf_op jit(solution)/shard_map/pallas_call | solution.py:261
  49.3 12.2 %shard_map.105 = (f32[2048,128]{1,0:T(8,128)}, f32[128,128]{1,0:T(8,128)}) custom-call(f32[2048,128]{1,0:T(8,128)S(1)} %get-tuple-element.4.image, f32[128,128]{1,0:T(8,128)S(1)} %bitcast.11), custom_call_target="tpu_custom_call" | custom-call | tf_op jit(solution)/shard_map/pallas_call | solution.py:358
  (2 shorter events, 0.0 us)
Async XLA Ops:
  0.6 10.7 %copy-start.2 = (s32[16]{0:T(128)S(1)}, s32[16]{0:T(128)}, u32[]{:S(2)}) copy-start(s32[16]{0:T(128)} %mrow.1) | copy-start | bytes 196
  0.6 10.7 %copy-start.1 = (bf16[2048,128]{1,0:T(8,128)(2,1)S(1)}, bf16[2048,128]{1,0:T(8,128)(2,1)}, u32[]{:S(2)}) copy-start(bf16[2048,128]{1,0:T(8,128)(2,1)} %param.9) | copy-start | bytes 1572868
  11.3 2.0 %copy-start = (bf16[32,7,64,64]{3,2,0,1:T(8,128)(2,1)S(1)}, bf16[32,7,64,64]{3,2,0,1:T(8,128)(2,1)}, u32[]{:S(2)}) copy-start(bf16[32,7,64,64]{3,2,0,1:T(8,128)(2,1)} %reshape.25) | copy-start | bytes 5505028
